TPU v7x, 128 devices: a whole 4x4x4 slice. The times are simulated.
128 devices in a mesh: grp: 4 (over z_lo, core), wide: 32 (over y, x, z_hi).
Axes of the slice: x: 4, y: 4, z: 4 (z_hi: 2, z_lo: 2; z = z_hi * 2 + z_lo), core: 2. Of those that a mesh axis runs over, the one named last changes fastest.
Arguments:
- student_feats: bfloat16 [128, 256, 1280], P(('grp', 'wide')), may hold values from -6 to 6
- dino_in: bfloat16 [128, 256, 1536], P('grp', 'wide'), may hold values from -6 to 6
- siglip_in: bfloat16 [128, 256, 1152], P('grp', 'wide'), may hold values from -6 to 6
- sam_in: bfloat16 [128, 1024, 1280], P('grp', 'wide'), may hold values from -6 to 6
- dino_proj: bfloat16 [1536, 1536], P(None, 'wide'), may hold values from -0.15625 to 0.15625
- siglip_proj: bfloat16 [1152, 1152], P(None, 'wide'), may hold values from -0.1875 to 0.1875
- sam_proj: bfloat16 [1280, 1280], P(None, 'wide'), may hold values from -0.15625 to 0.15625
- dino_index: int32 [128, 256], P(('grp', 'wide')), may hold values from 0 to 255, as said below
- siglip_index: int32 [128, 256], P(('grp', 'wide')), may hold values from 0 to 255, as said below
- sam_index: int32 [128, 256], P(('grp', 'wide')), may hold values from 0 to 255, as said below
- dino_first: bfloat16 [1280, 640], P('wide'), may hold values from -0.15625 to 0.15625
- dino_second: bfloat16 [640, 1536], P('wide'), may hold values from -0.25 to 0.25
- siglip_first: bfloat16 [1280, 640], P('wide'), may hold values from -0.15625 to 0.15625
- siglip_second: bfloat16 [640, 1152], P('wide'), may hold values from -0.25 to 0.25
- sam_first: bfloat16 [1280, 640], P('wide'), may hold values from -0.15625 to 0.15625
- sam_second: bfloat16 [640, 1280], P('wide'), may hold values from -0.25 to 0.25
Outputs:
- dino_first_grad: float32 [1280, 640], P('wide')
- dino_second_grad: float32 [640, 1536], P('wide')
- siglip_first_grad: float32 [1280, 640], P('wide')
- siglip_second_grad: float32 [640, 1152], P('wide')
- sam_first_grad: float32 [1280, 640], P('wide')
- sam_second_grad: float32 [640, 1280], P('wide')
Inputs may be any that keep to these rules, and one draw needn't show every extreme that they name: dino_index[i, s] is the cell of the 16 x 16 grid under student patch s of image i, after that image's optional left-right mirror. siglip_index[i, s] is the cell of the 16 x 16 grid under student patch s of image i, after that image's optional left-right mirror. sam_index[i, s] is the block of the 16 x 16 grid of SAM blocks under student patch s of image i, after that image's optional left-right mirror.
All inputs are finite; a program needn't handle non-finite values.
Results may differ from a plain program's by a relative error of at most 0.002.
Values may be sent and summed in bfloat16 or wider, within the bound.
A program may use at most 128 MiB of HBM per device.

v0:
```python
import functools
import itertools
import math

import jax
import jax.numpy as jnp
from jax import lax
from jax.experimental import pallas as pl
from jax.experimental.pallas import tpu as pltpu
from jax.sharding import PartitionSpec as P

MESH = pl.DeviceIdType.MESH
LANE = 128
ALL = (0, 4)
BOTH = (0, 2)


def layer_norm(values, count=None, mask=None):
    count = values.shape[-1] if count is None else count
    centered = values - jnp.sum(values, axis=-1, keepdims=True) * (1.0 / count)
    if mask is not None:
        centered = centered * mask
    variance = jnp.sum(centered * centered, axis=-1, keepdims=True) * (1.0 / count)
    return centered * lax.rsqrt(variance + 1e-05)


def gelu_pair(act):
    cdf = 0.5 * (1.0 + jax.scipy.special.erf(act * (1.0 / math.sqrt(2.0))))
    density = jnp.exp(-0.5 * act * act) * (1.0 / math.sqrt(2.0 * math.pi))
    return (act * cdf, cdf + act * density)


class Place:
    def __init__(self):
        grp, wide = lax.axis_index("grp"), lax.axis_index("wide")
        self.grp, self.wide = grp, wide
        self.z_lo, self.core = grp // 2, grp % 2
        self.y, self.x, self.z_hi = wide // 8, wide // 2 % 4, wide % 2

    def x_next(self, step):
        return (self.grp, (self.y * 4 + self.x_at(step)) * 2 + self.z_hi)

    def y_next(self, step):
        return (self.grp, (self.y_at(step) * 4 + self.x) * 2 + self.z_hi)

    def x_at(self, step):
        return (self.x + step + 4) % 4

    def y_at(self, step):
        return (self.y + step + 4) % 4

    def mirror_z(self):
        return ((1 - self.z_lo) * 2 + self.core, (self.y * 4 + self.x) * 2 + 1 - self.z_hi)

    def next_z(self):
        return ((1 - self.z_lo) * 2 + self.core, self.wide)

    def sibling(self):
        return (self.z_lo * 2 + 1 - self.core, self.wide)


def enter(partners):
    barrier = pltpu.get_barrier_semaphore()
    for partner in partners:
        pl.semaphore_signal(barrier, inc=1, device_id=partner, device_id_type=MESH)
    pl.semaphore_wait(barrier, len(partners))


def part(entry):
    return pl.ds(entry[0], entry[1]) if isinstance(entry, tuple) else entry


def extent(entry):
    return entry[1] if isinstance(entry, tuple) else None


class Copies:
    def __init__(self, send_sem, recv_sem):
        self.send_sem, self.recv_sem = send_sem, recv_sem
        self.started = []

    def send(self, src, dst, device):
        i = len(self.started)
        if i >= SENDS:
            self.started[i - SENDS].wait_send()
        copy = pltpu.make_async_remote_copy(
            src_ref=src,
            dst_ref=dst,
            send_sem=self.send_sem.at[i % SENDS],
            recv_sem=self.recv_sem.at[i],
            device_id=device,
            device_id_type=MESH,
        )
        copy.start()
        self.started.append(copy)
        return copy

    def finish(self):
        for copy in self.started[-SENDS:]:
            copy.wait_send()


class Task:
    def __init__(self, link, cost, needs, run, rank=0):
        self.link, self.cost, self.run, self.rank = link, cost, run, rank
        self.needs = [need for need in needs if need is not None]
        self.copy, self.landed, self.done = None, False, None


BACKLOG = 2.0
LATENCY = 3.0
RATES = {"sibling": 0.4, "local": 0.65}


def span(task):
    return task.cost if task.link == "core" else task.cost * 1e-6 / RATES.get(task.link, 0.0445)


def plan(tasks):
    tails = {id(task): 0.0 for task in tasks}
    for task in reversed(tasks):
        tail = tails[id(task)] + span(task) + (0.0 if task.link == "core" else 1.5)
        for need in task.needs:
            tails[id(need)] = max(tails[id(need)], tail)
    free, now, order, left = {}, 0.0, [], list(tasks)
    while left:
        best = None
        for task in left:
            ready = 0.0
            for need in task.needs:
                if need.done is None:
                    break
                ready = max(ready, need.done)
            else:
                if task.link != "core":
                    ready = max(ready, free.get(task.link, 0.0) - BACKLOG)
                key = (max(ready, now), task.link == "core", task.rank, -tails[id(task)])
                if best is None or key < best[0]:
                    best = (key, task)
        (now, *_), task = best
        if task.link == "core":
            now += task.cost
            task.done = now
        else:
            now += 0.03
            free[task.link] = max(now, free.get(task.link, 0.0)) + span(task)
            task.done = free[task.link] + LATENCY
        order.append(task)
        left.remove(task)
    return order


def carry_out(order):
    for task in order:
        for need in task.needs:
            land(need)
        task.copy = task.run()
    for task in order:
        land(task)


def land(task):
    if task.copy is not None and not task.landed:
        if task.link == "local":
            task.copy.wait()
        else:
            task.copy.wait_recv()
        task.landed = True


WIDTHS = (1536, 1280, 1280)
STUDENT = 1280 + LANE
PROJ_SPLITS = ((2, 1, 2, 1), (1, 2, 1, 1), (1, 1, 1, 2))
FIRST_SPLITS = ((1, 1, 1, 0), (1, 1, 0, 1), (1, 0, 1, 1))
SECOND_SPLITS = ((1, 2, 1, 2), (1, 1, 2, 1), (1, 2, 1, 1))
GRAD_SPLITS = (
    ((1, 0, 1, 1), (0, 1, 1, 1), (1, 1, 1, 0)),
    ((1, 1, 2, 2), (1, 1, 1, 2), (1, 1, 2, 1)),
)
COPIES = 646
SENDS = 48
ORDER = (2, 0, 1)
EARLY = 1
LOCALS = 24


def cut_y(region, half):
    return ((half * 2, 2), region[1], region[2])


def cut_x(region, half):
    return (region[0], (half * 2, 2), region[2])


def cut_z(region, half):
    return (region[0], region[1], half)


def chunks(region):
    return math.prod(extent(entry) or 1 for entry in region)


class Refs:
    def __init__(self, refs):
        self.refs = list(refs)

    def take(self, count):
        taken, self.refs = self.refs[:count], self.refs[count:]
        return taken


def kernel(factor, *refs):
    refs = Refs(refs)
    shards, inputs, (feats, flags_in) = refs.take(9), refs.take(3), refs.take(2)
    outs, weights = refs.take(6), refs.take(6)
    hop_y, ((rows_y,), hop_x, (rows_all,), hop_z) = refs.take(2), (
        refs.take(1),
        refs.take(2),
        refs.take(1),
        refs.take(2),
    )
    projs, (first_all, second_all, rows_in) = refs.take(3), refs.take(3)
    whole = projs + weights
    held, targets = refs.take(3), refs.take(3)
    (act, pred, slope) = refs.take(3)
    normed, normed_too, hidden, hidden_too = (refs.take(3) for _ in range(4))
    grad_act, grad_act_too, grad_pred, grad_pred_too = (refs.take(3) for _ in range(4))
    cells = grad_pred[2]
    sums, last = refs.take(6), refs.take(6)
    (student_in,) = refs.take(1)
    spare, (local_sem, send_sem, recv_sem) = iter(refs.refs[:-3]), refs.refs[-3:]
    at = Place()
    student_in[:, :, :, :1280] = (
        layer_norm(feats[...].astype(jnp.float32))
        .astype(jnp.bfloat16)
        .reshape(4, 4, 16, 1280)
    )
    student_in[:, :, :, 1280:] = flags_in[...].reshape(4, 4, 16, LANE)
    enter(
        [
            at.x_next(1),
            at.x_next(-1),
            at.y_next(1),
            at.y_next(-1),
            at.mirror_z(),
            at.next_z(),
            at.sibling(),
        ]
    )
    copies = Copies(send_sem, recv_sem)
    locals_used = itertools.count()
    tasks = []
    own = (at.y, at.x, at.z_hi)

    def add_task(*args):
        tasks.append(Task(*args))
        return tasks[-1]

    def size_of(ref):
        return math.prod(ref.shape) * 2

    def move(src, dst, needs, rank):
        def run():
            copy = pltpu.make_async_copy(src, dst, local_sem.at[next(locals_used)])
            copy.start()
            return copy

        return add_task("local", size_of(dst), needs, run, rank)

    def carry(src, dst, link, device, needs, rank):
        def run():
            return copies.send(src, dst, device)

        return add_task(link, size_of(dst), needs, run, rank)

    def spread_student():
        x_low, x_high = pl.ds(0, 2), pl.ds(2, 2)
        here = move(student_in.at[at.y], rows_y.at[at.y], [], EARLY)
        got = [here]
        got.append(
            carry(student_in.at[at.y_at(1)], rows_y.at[at.y], "y+", at.y_next(1), [], EARLY)
        )
        got.append(
            carry(student_in.at[at.y_at(-1)], rows_y.at[at.y], "y-", at.y_next(-1), [], EARLY)
        )
        far = student_in.at[at.y_at(2)]
        up = carry(far.at[x_low], hop_y[0], "y+", at.y_next(1), [], EARLY)
        down = carry(far.at[x_high], hop_y[1], "y-", at.y_next(-1), [], EARLY)
        got.append(
            carry(hop_y[0], rows_y.at[at.y_at(-1), x_low], "y+", at.y_next(1), [up], EARLY)
        )
        got.append(
            carry(hop_y[1], rows_y.at[at.y_at(1), x_high], "y-", at.y_next(-1), [down], EARLY)
        )

        every, low, high = pl.ds(0, 4), pl.ds(0, 2), pl.ds(2, 2)
        mine = rows_all.at[every, at.x, at.z_hi]
        done = [move(rows_y.at[every, at.x], mine, got, EARLY)]
        for step, link in ((1, "x+"), (-1, "x-")):
            src = rows_y.at[every, at.x_at(step)]
            done.append(carry(src, mine, link, at.x_next(step), got, EARLY))
        far = at.x_at(2)
        up = carry(rows_y.at[low, far], hop_x[0], "x+", at.x_next(1), got, EARLY)
        down = carry(rows_y.at[high, far], hop_x[1], "x-", at.x_next(-1), got, EARLY)
        dst = rows_all.at[low, at.x_at(-1), at.z_hi]
        done.append(carry(hop_x[0], dst, "x+", at.x_next(1), [up], EARLY))
        dst = rows_all.at[high, at.x_at(1), at.z_hi]
        done.append(carry(hop_x[1], dst, "x-", at.x_next(-1), [down], EARLY))

        landed = []
        for i in range(2):
            one, two = pl.ds(i, 1), pl.ds(2 + i, 1)
            src = rows_all.at[one, every, at.z_hi]
            first = carry(src, hop_z[0].at[one], "mirror", at.mirror_z(), done, EARLY)
            src = rows_all.at[two, every, at.z_hi]
            second = carry(src, hop_z[1].at[one], "next", at.next_z(), done, EARLY)
            dst = rows_all.at[one, every, 1 - at.z_hi]
            src = hop_z[0].at[one]
            landed.append(carry(src, dst, "next", at.next_z(), [first], EARLY))
            dst = rows_all.at[two, every, at.z_hi]
            src = hop_z[1].at[one]
            landed.append(carry(src, dst, "mirror", at.mirror_z(), [second], EARLY))
        return move(rows_all, rows_in, done + landed, EARLY)

    def gather(k, splits, rank):
        shard, array = shards[k], whole[k]
        found = []

        def lanes(s):
            start = at.core * sum(splits) + sum(splits[:s])
            return pl.ds(pl.multiple_of(start * LANE, LANE), splits[s] * LANE)

        def view(s, region):
            return array.at[part(region[0]), part(region[1]), part(region[2]), :, lanes(s)]

        def send(s, region, link, device, needs):
            src = shard.at[:, lanes(s)] if region is own else view(s, region)
            return carry(src, view(s, region), link, device, needs, rank)

        def share(s, region, needs):
            found.append(send(s, region, "sibling", at.sibling(), needs))

        def across(s):
            return [kept, send(s, own, "mirror", at.mirror_z(), [])]

        def across_both(s, needs):
            mine, other = (2 * at.z_lo, 2), (2 - 2 * at.z_lo, 2)
            share(s, (ALL, ALL, at.z_hi), needs)
            one = send(s, (other, ALL, at.z_hi), "mirror", at.mirror_z(), needs)
            two = send(s, (mine, ALL, 1 - at.z_hi), "next", at.next_z(), [one])
            share(s, (mine, ALL, 1 - at.z_hi), [one])
            share(s, (other, ALL, 1 - at.z_hi), [two])
            found.extend(needs + [one, two])

        def last_around(s, axis, block, cut, needs):
            place = at.x_at if axis == "x" else at.y_at
            share(s, block(place(0)), needs)
            up, down, one, two = around(s, axis, block, cut, needs)[len(needs) :]
            share(s, block(place(-1)), [up])
            share(s, block(place(1)), [down])
            share(s, block(place(2)), [one, two])
            found.extend(needs + [up, down, one, two])

        def around(s, axis, block, cut, needs):
            place, device = (at.x_at, at.x_next) if axis == "x" else (at.y_at, at.y_next)
            here = own if cut is None else block(place(0))
            back, ahead = block(place(-1)), block(place(1))
            up = send(s, here, axis + "+", device(1), needs)
            down = send(s, here, axis + "-", device(-1), needs)
            got = needs + [up, down]
            if cut is not None:
                got.append(send(s, cut(back, 0), axis + "+", device(1), [up]))
                got.append(send(s, cut(ahead, 1), axis + "-", device(-1), [down]))
            elif k % 2 == 0:
                got.append(send(s, back, axis + "+", device(1), [up]))
            else:
                got.append(send(s, ahead, axis + "-", device(-1), [down]))
            return got

        def keep():
            start = pl.multiple_of(at.core * sum(splits) * LANE, LANE)
            columns = pl.ds(start, sum(splits) * LANE)
            return move(shard.at[:, columns], array.at[own + (slice(None), columns)], [], -1)

        kept = keep()
        found.append(kept)
        if splits[0]:
            got = around(0, "y", lambda c: (c, at.x, BOTH), cut_z, across(0))
            last_around(0, "x", lambda c: (ALL, c, BOTH), cut_y, got)
        if splits[1]:
            got = around(1, "x", lambda c: (at.y, c, BOTH), cut_z, across(1))
            last_around(1, "y", lambda c: (c, ALL, BOTH), cut_x, got)
        if splits[2]:
            got = [kept] + around(2, "x", lambda c: (at.y, c, at.z_hi), None, [])
            got = around(2, "y", lambda c: (c, ALL, at.z_hi), cut_x, got)
            across_both(2, got)
        if splits[3]:
            got = [kept] + around(3, "y", lambda c: (c, at.x, at.z_hi), None, [])
            got = around(3, "x", lambda c: (ALL, c, at.z_hi), cut_y, got)
            across_both(3, got)
        return found

    def mix(rows_ref, begin, weights, count, mask, write):
        rows = rows_ref[begin : begin + 256, :]
        width = rows.shape[1]
        step = width // 2
        for half in range(2):
            block = weights[2 * half : 2 * half + 2]
            mixed = lax.dot_general(
                rows,
                block.reshape(step, width),
                (((1,), (1,)), ((), ())),
                preferred_element_type=jnp.float32,
            )
            side = rows[:, half * step : (half + 1) * step].astype(jnp.float32)
            pred[:, half * step : (half + 1) * step] = side + mixed

        @pl.loop(0, 2)
        def _(i):
            spot = pl.ds(pl.multiple_of(i * 128, 128), 128)
            values = pred[spot, :width]
            write(spot, layer_norm(values, count, mask).astype(jnp.bfloat16))

    def dino():
        def write(spot, values):
            targets[0][spot, :] = values

        mix(held[0], 0, projs[0], 1536, None, write)

    def siglip():
        def write(spot, values):
            targets[1][spot, :] = values

        column = lax.broadcasted_iota(jnp.int32, (1, 1280), 1)
        mask = (column % 40 < 36).astype(jnp.float32)
        mix(held[1], 0, projs[1], 1152, mask, write)

    def sam(b):
        def run():
            def write(spot, values):
                cells[spot, :] = values

            mix(held[2], b * 256, projs[2], 1280, None, write)
            block = lax.broadcasted_iota(jnp.int32, (64, 256), 0)
            cell = lax.broadcasted_iota(jnp.int32, (64, 256), 1)
            member = ((cell >= 4 * block) & (cell < 4 * block + 4)).astype(jnp.bfloat16)
            total = jnp.dot(member, cells[...], preferred_element_type=jnp.float32)
            targets[2][b * 64 : b * 64 + 64, :] = (total * 0.25).astype(jnp.bfloat16)

        return run

    def pick(t):
        rows = rows_in[...].reshape(512, STUDENT)
        spot = lax.broadcasted_iota(jnp.int32, (256, 512), 0)
        source = lax.broadcasted_iota(jnp.int32, (256, 512), 1)
        column = at.z_hi * 8 + spot % 8
        straight = spot // 8 * 16 + column
        flags = jnp.dot(
            (source == straight).astype(jnp.bfloat16),
            rows[:, 1280:],
            preferred_element_type=jnp.float32,
        )
        shift = jnp.where(flags[:, t : t + 1] > 0.5, 0, 15 - 2 * column)
        normed[t][...] = jnp.dot(
            (source == straight + shift).astype(jnp.bfloat16),
            rows[:, :1280],
            preferred_element_type=jnp.float32,
        ).astype(jnp.bfloat16)

    def forward(t):
        def run():
            pick(t)
            act[...] = jnp.dot(
                normed[t][...],
                first_all[...].reshape(1280, 768),
                preferred_element_type=jnp.float32,
            )

            @pl.loop(0, 8)
            def _(i):
                spot = pl.ds(pl.multiple_of(i * 32, 32), 32)
                hid, tilt = gelu_pair(act[spot, :])
                hidden[t][spot, :] = hid.astype(jnp.bfloat16)
                slope[spot, :] = tilt

        return run

    def backward(t):
        width = WIDTHS[t]

        def run():
            second = second_all[:, :, :, :, :width].reshape(768, width)
            pred[:, :width] = jnp.dot(
                hidden[t][...], second, preferred_element_type=jnp.float32
            )

            @pl.loop(0, 8)
            def _(i):
                spot = pl.ds(pl.multiple_of(i * 32, 32), 32)
                wanted = targets[t][spot, :].astype(jnp.float32)
                grad = factor * (pred[spot, :width] - wanted)
                grad_pred[t][spot, :] = grad.astype(jnp.bfloat16)

            act[...] = lax.dot_general(
                grad_pred[t][...],
                second,
                (((1,), (1,)), ((), ())),
                preferred_element_type=jnp.float32,
            )

            @pl.loop(0, 8)
            def _(i):
                spot = pl.ds(pl.multiple_of(i * 32, 32), 32)
                grad_act[t][spot, :] = (act[spot, :] * slope[spot, :]).astype(jnp.bfloat16)

        return run

    def half_of(width, core):
        return pl.ds(pl.multiple_of(core * (width // 2), LANE), width // 2)

    def outer(left, right):
        return lax.dot_general(
            left, right, (((0,), (0,)), ((), ())), preferred_element_type=jnp.float32
        )

    def gradient(out, left, left_too, right, right_too):
        def run():
            mine, other = right[:, half_of(right.shape[1], at.core)], right_too[...]
            step = left.shape[1] // 2
            for side in range(2):
                columns = slice(step * side, step * side + step)
                total = outer(left[:, columns], mine) + outer(left_too[:, columns], other)
                out[2 * side : 2 * side + 2] = total.reshape((2,) + out.shape[1:])

        return run

    def reduce(k, splits, needs, rank):
        array = sums[k]
        depth = array.shape[3]

        def lanes(s):
            return pl.ds(sum(splits[:s]) * LANE, splits[s] * LANE)

        def view(s, region):
            return array.at[part(region[0]), part(region[1]), part(region[2]), :, lanes(s)]

        def send(s, region, link, device, needs):
            room = next(spare)

            def run():
                return copies.send(view(s, region), room, device)

            size = chunks(region) * depth * splits[s] * LANE * 4
            task = add_task(link, size, needs, run, rank)
            task.room = room
            return task

        def add(s, region, sent, needs):
            sizes = [extent(entry) for entry in region]

            def run():
                for spots in itertools.product(*[range(size or 1) for size in sizes]):
                    there = tuple(spot for spot, size in zip(spots, sizes) if size)
                    where = tuple(
                        spot + entry[0] if size else entry
                        for spot, size, entry in zip(spots, sizes, region)
                    ) + (slice(None), lanes(s))
                    total = array[where]
                    for task in sent:
                        total = total + task.room[there + (slice(None), slice(None))]
                    array[where] = total

            size = chunks(region) * depth * splits[s] * LANE * 4
            return add_task("core", 0.03 + size * 0.06e-6, sent + needs, run, -1)

        def across(s, needs):
            sent = send(s, (at.y, at.x, 1 - at.z_hi), "mirror", at.mirror_z(), needs)
            return [add(s, own, [sent], needs)]

        def across_both(s, needs):
            mine, other = (2 * at.z_lo, 2), (2 - 2 * at.z_lo, 2)
            sent = send(s, (other, ALL, 1 - at.z_hi), "next", at.next_z(), needs)
            added = add(s, (mine, ALL, 1 - at.z_hi), [sent], needs)
            sent = send(s, (mine, ALL, 1 - at.z_hi), "mirror", at.mirror_z(), [added])
            return [add(s, (other, ALL, at.z_hi), [sent], needs)]

        def around(s, axis, block, cut, needs):
            place, device = (at.x_at, at.x_next) if axis == "x" else (at.y_at, at.y_next)
            here, over, back, ahead = (block(place(step)) for step in (0, 2, -1, 1))
            up, down = [], []
            if cut is not None:
                sent = send(s, cut(over, 0), axis + "+", device(1), needs)
                up.append(add(s, cut(ahead, 0), [sent], needs))
                sent = send(s, cut(over, 1), axis + "-", device(-1), needs)
                down.append(add(s, cut(back, 1), [sent], needs))
            elif k % 2 == 0:
                sent = send(s, over, axis + "+", device(1), needs)
                up.append(add(s, ahead, [sent], needs))
            else:
                sent = send(s, over, axis + "-", device(-1), needs)
                down.append(add(s, back, [sent], needs))
            one = send(s, ahead, axis + "+", device(1), needs + up)
            two = send(s, back, axis + "-", device(-1), needs + down)
            return [add(s, here, [one, two], needs)]

        def settle(needs):
            mine = half_of(outs[k].shape[1], at.core)

            def swap():
                return copies.send(array.at[own], last[k], at.next_z())

            def total():
                outs[k][:, mine] = array[own] + last[k][...]

            def share_total():
                return copies.send(outs[k].at[:, mine], outs[k].at[:, mine], at.sibling())

            size = depth * sum(splits) * LANE * 4
            swapped = add_task("next", size, needs, swap, -1)
            added = add_task("core", 0.1, needs + [swapped], total, -1)
            add_task("sibling", size, [added], share_total, -1)

        done = []
        if splits[0]:
            got = around(0, "x", lambda c: (ALL, c, BOTH), cut_y, needs)
            got = around(0, "y", lambda c: (c, at.x, BOTH), cut_z, got)
            done += across(0, got)
        if splits[1]:
            got = around(1, "y", lambda c: (c, ALL, BOTH), cut_x, needs)
            got = around(1, "x", lambda c: (at.y, c, BOTH), cut_z, got)
            done += across(1, got)
        if splits[2]:
            got = across_both(2, needs)
            got = around(2, "y", lambda c: (c, ALL, at.z_hi), cut_x, got)
            done += around(2, "x", lambda c: (at.y, c, at.z_hi), None, got)
        if splits[3]:
            got = across_both(3, needs)
            got = around(3, "x", lambda c: (ALL, c, at.z_hi), cut_y, got)
            done += around(3, "y", lambda c: (c, at.x, at.z_hi), None, got)
        settle(done)

    loaded = [move(inputs[t], held[t], [], 10 * ORDER.index(t) + 3) for t in range(3)]
    rows_ready = None
    before = None
    for place, t in enumerate(ORDER):
        rank = 10 * place
        projected = gather(t, PROJ_SPLITS[t], rank)
        needs = projected + [loaded[t]]
        if t == 0:
            mapped = [add_task("core", 2.0, needs, dino, rank + 1)]
        elif t == 1:
            mapped = [add_task("core", 1.7, needs, siglip, rank + 1)]
        else:
            mapped = [add_task("core", 1.8, needs, sam(b), rank + 1) for b in range(4)]
        if rows_ready is None:
            rows_ready = spread_student()
        first = gather(3 + t, FIRST_SPLITS[t], rank + 1)
        second = gather(6 + t, SECOND_SPLITS[t], rank + 2)
        free = [before] if before else []
        ahead = [forwarded] if before else []
        first = move(whole[3 + t], first_all, first + ahead, rank)
        second = move(
            whole[6 + t], second_all.at[:, :, :, :, pl.ds(0, WIDTHS[t])], second + free, rank
        )
        forwarded = add_task("core", 2.1, [rows_ready, first] + free, forward(t), rank + 3)

        def share(src, dst, needs, rank=rank):
            if src.shape[1] != dst.shape[1]:
                src = src.at[:, half_of(src.shape[1], 1 - at.core)]
            return carry(src, dst, "sibling", at.sibling(), needs, rank)

        got_normed = share(normed[t], normed_too[t], [forwarded])
        got_hidden = share(hidden[t], hidden_too[t], [forwarded])
        before = add_task("core", 2.1, [second, forwarded] + mapped, backward(t), rank + 3)
        got_act = share(grad_act[t], grad_act_too[t], [before])
        got_pred = share(grad_pred[t], grad_pred_too[t], [before])
        run = gradient(sums[t], normed[t], normed_too[t], grad_act[t], grad_act_too[t])
        done = add_task("core", 0.6, [before, got_normed, got_act], run, rank + 2)
        reduce(t, GRAD_SPLITS[0][t], [done], 40 + place)
        run = gradient(sums[3 + t], hidden[t], hidden_too[t], grad_pred[t], grad_pred_too[t])
        done = add_task("core", 0.7, [before, got_hidden, got_pred], run, rank + 2)
        reduce(3 + t, GRAD_SPLITS[1][t], [done], 40 + place)
    carry_out(plan(tasks))
    copies.finish()


def distil(shards, inputs, feats, flags, factor):
    inside = pl.BlockSpec(memory_space=pltpu.VMEM)
    outside = pl.BlockSpec(memory_space=pl.ANY)
    depth = [40] * 3 + [24] * 3
    width = [384] * 3 + [w // 2 for w in WIDTHS]
    splits = GRAD_SPLITS[0] + GRAD_SPLITS[1]

    def rooms():
        plane, line = [(2, 2), (2, 2), (4, 2), (4, 2)], [(), (), (2,), (2,)]
        column, spot = [(2,), (2,), (4,), (4,)], [(), (), ()]
        leads = [plane + line + [()]] * 2 + [[(2, 4), (2, 4)] + column + spot] * 2
        for t in ORDER:
            for k in (t, 3 + t):
                for s in range(4):
                    if splits[k][s]:
                        for lead in leads[s]:
                            yield pltpu.VMEM(lead + (depth[k], splits[k][s] * LANE), jnp.float32)

    def half_wide(*shape):
        return jax.ShapeDtypeStruct(shape, jnp.bfloat16)

    def table(*shape):
        return pltpu.VMEM(shape, jnp.bfloat16)

    def three(*widths):
        return [table(256, w) for w in widths]

    outs = [jax.ShapeDtypeStruct((d, 2 * w), jnp.float32) for d, w in zip(depth, width)]
    landings = [half_wide(4, 4, 2, *shard.shape) for shard in shards[3:]] + [
        half_wide(2, 16, STUDENT),
        half_wide(2, 16, STUDENT),
        half_wide(4, 4, 16, STUDENT),
        half_wide(2, 16, STUDENT),
        half_wide(2, 16, STUDENT),
        half_wide(4, 4, 2, 16, STUDENT),
        half_wide(2, 4, 16, STUDENT),
        half_wide(2, 4, 16, STUDENT),
    ]
    results = pl.pallas_call(
        functools.partial(kernel, factor),
        out_shape=outs + landings,
        in_specs=[outside] * (len(shards) + len(inputs)) + [inside] * 2,
        out_specs=[inside] * len(outs) + [outside] * len(landings),
        scratch_shapes=[
            table(4, 4, 2, 48, 1536),
            table(4, 4, 2, 40, 1280),
            table(4, 4, 2, 40, 1280),
            table(4, 4, 2, 40, 768),
            table(4, 4, 2, 24, 1536),
            table(4, 4, 2, 16, STUDENT),
            *[table(*rows.shape) for rows in inputs],
            *three(*WIDTHS),
            pltpu.VMEM((256, 768), jnp.float32),
            pltpu.VMEM((256, 1536), jnp.float32),
            pltpu.VMEM((256, 768), jnp.float32),
            *three(*[1280] * 6),
            *three(*[768] * 6),
            *three(*[768] * 3),
            *three(*[384] * 3),
            *three(*WIDTHS),
            *three(*[w // 2 for w in WIDTHS]),
            *[pltpu.VMEM((4, 4, 2, d, w), jnp.float32) for d, w in zip(depth, width)],
            *[pltpu.VMEM((d, w), jnp.float32) for d, w in zip(depth, width)],
            table(4, 4, 16, STUDENT),
            *rooms(),
            pltpu.SemaphoreType.DMA((LOCALS,)),
            pltpu.SemaphoreType.DMA((SENDS,)),
            pltpu.SemaphoreType.DMA((COPIES,)),
        ],
        compiler_params=pltpu.CompilerParams(
            collective_id=0, has_side_effects=True, vmem_limit_bytes=63 * 1024 * 1024
        ),
        name="distil",
    )(*shards, *inputs, feats, flags)
    return results[: len(outs)]


def spread(width, group, room):
    rows = lax.broadcasted_iota(jnp.int32, (width, width // group * room), 0)
    columns = lax.broadcasted_iota(jnp.int32, (width, width // group * room), 1)
    return (rows // group * room + rows % group == columns).astype(jnp.bfloat16)


def place_columns(values, table):
    return jnp.dot(values, table, preferred_element_type=jnp.float32).astype(jnp.bfloat16)


def mirror_flags(indices):
    patches = jnp.arange(256, dtype=jnp.int32)
    flags = jnp.stack([index[0] == patches for index in indices], axis=-1).astype(jnp.bfloat16)
    return jnp.pad(flags, ((0, 0), (0, LANE - 3)))


def body(
    student_feats,
    dino_in,
    siglip_in,
    sam_in,
    dino_proj,
    siglip_proj,
    sam_proj,
    dino_index,
    siglip_index,
    sam_index,
    dino_first,
    dino_second,
    siglip_first,
    siglip_second,
    sam_first,
    sam_second,
):
    images_total = student_feats.shape[0] * 128
    siglip_room = spread(1152, 36, 40)
    hidden_room = spread(640, 20, 24)
    siglip_turned = jnp.pad(place_columns(siglip_proj.T, siglip_room), ((0, 4), (0, 0)))
    firsts = place_columns(
        jnp.concatenate([dino_first, siglip_first, sam_first], axis=0), hidden_room
    ).reshape(3, 40, 768)
    seconds = [
        jnp.pad(second, ((0, 4), (0, 0)))
        for second in (dino_second, place_columns(siglip_second, siglip_room), sam_second)
    ]
    sums = distil(
        [dino_proj.T, siglip_turned, sam_proj.T, *firsts, *seconds],
        [
            dino_in.reshape(256, -1),
            place_columns(siglip_in.reshape(256, -1), siglip_room),
            sam_in.reshape(1024, -1),
        ],
        student_feats[0],
        mirror_flags((dino_index, siglip_index, sam_index)),
        2.0 / images_total,
    )
    firsts = [total.reshape(40, 32, 24)[..., :20].reshape(40, 640) for total in sums[:3]]
    seconds = [total[:20] for total in sums[3:]]
    siglip_two = seconds[1].reshape(20, 32, 40)[..., :36].reshape(20, 1152)
    return (firsts[0], seconds[0], firsts[1], siglip_two, firsts[2], seconds[2])


def solution(mesh):
    shared = P("wide", None)
    return jax.shard_map(
        body,
        mesh=mesh,
        in_specs=(
            P(("grp", "wide"), None, None),
            *[P("grp", "wide", None)] * 3,
            *[P(None, "wide")] * 3,
            *[P(("grp", "wide"), None)] * 3,
            *[shared] * 6,
        ),
        out_specs=(shared,) * 6,
        check_vma=False,
    )
```

profile of v0, /device:TPU:1, one launch (start us, length us, event | category | flops | bytes accessed | tf_op | source)
XLA Modules:
  0.0 179.2 jit_solution(12958220352274216167)
XLA Ops:
  0.6 0.0 copy-start
  0.6 0.7 bitcast_compare_fusion.2
  1.4 0.7 bitcast_compare_fusion
  2.2 0.2 copy.34
  2.4 0.7 pad_convert_fusion.refs_13_
  3.0 0.0 copy-start.6
  3.0 0.0 copy-start.5
  3.0 0.0 copy-start.7
  3.0 2.2 %fusion.2 = bf16[20,1280]{1,0:T(8,128)(2,1)S(1)} fusion(bf16[20,1152]{1,0:T(8,128)(2,1)} %param.29, s32[1152]{0:T(1024)S(1)} %get-tuple-element.34, s32[1152]{0:T(1024)S(1)} %get-tuple-element.35, s32[1152]{0:T(1024)S(1)} %get-tuple-element.33, s32[1152]{0:T(1024)S(1)} %get-tuple-element.36, pred[1152]{0:T(1024)(128)(4,1)S(1)} %get-tuple-element.37, ...), kind=kOutput, calls=%fused_computation.6 | convolution fusion | flops 66380800 | bytes 118016 | tf_op jit(solution)/shard_map/dot_general | solution.py:771
  5.2 0.6 pad.23.refs_7_
  5.9 0.0 copy-done.6
  5.9 0.6 pad.24.refs_8_
  6.5 0.0 copy-done.5
  6.5 0.6 pad.22.refs_6_
  7.2 0.0 copy-done.7
  7.2 0.0 copy-start.8
  7.2 0.0 copy-start.9
  7.2 0.0 copy-start.10
  7.2 1.4 fusion.1
  8.6 0.7 pad.21.refs_1_
  9.2 0.0 copy-done.8
  9.2 0.0 copy-done.9
  9.2 0.0 copy-done.10
  9.2 0.8 fusion.4
  10.1 0.7 fusion.32
  10.7 0.0 copy-done
  10.7 2.5 %fusion.refs_10_ = bf16[256,1280]{1,0:T(8,128)(2,1)} fusion(bf16[32,8,1152]{2,1,0:T(8,128)(2,1)S(1)} %copy-done, s32[1152]{0:T(1024)S(1)} %get-tuple-element.34, s32[1152]{0:T(1024)S(1)} %get-tuple-element.35, s32[1152]{0:T(1024)S(1)} %get-tuple-element.33, s32[1152]{0:T(1024)S(1)} %get-tuple-element.36, pred[1152]{0:T(1024)(128)(4,1)S(1)} %get-tuple-element.37, ...), kind=kOutput, calls=%fused_computation.2 | convolution fusion | flops 762675200 | bytes 1265920 | tf_op jit(solution)/shard_map/dot_general | solution.py:771
  13.3 158.7 %distil.1 = (f32[40,768]{1,0:T(8,128)}, f32[40,768]{1,0:T(8,128)}, f32[40,768]{1,0:T(8,128)}, f32[24,1536]{1,0:T(8,128)}, f32[24,1280]{1,0:T(8,128)}, /*index=5*...) custom-call(bf16[48,1536]{1,0:T(8,128)(2,1)} %bitcast.45, ...), custom_call_target="tpu_custom_call" | custom-call | tf_op jit(solution)/shard_map/distil/pallas_call | solution.py:725
  172.0 0.0 copy-start.4
  172.0 0.0 copy-start.3
  172.0 1.1 copy.35
  173.1 0.0 copy-start.1
  173.1 0.0 copy-start.2
  173.1 0.8 copy.38
  173.9 1.1 reshape.101
  175.1 0.9 reshape.102
  175.9 0.0 copy-done.4
  175.9 0.2 copy.36
  176.1 0.8 copy.39
  176.9 0.0 copy-done.3
  176.9 0.2 copy.37
  177.1 0.8 copy.40
  177.9 0.0 copy-done.1
  177.9 0.7 copy.44
  178.6 0.0 copy-done.2
  178.6 0.6 copy.45
  (10 shorter events, 0.2 us)
Async XLA Ops:
  0.6 10.1 %copy-start = (bf16[32,8,1152]{2,1,0:T(8,128)(2,1)S(1)}, bf16[32,8,1152]{2,1,0:T(8,128)(2,1)}, u32[]{:S(2)}) copy-start(bf16[32,8,1152]{2,1,0:T(8,128)(2,1)} %param.18) | copy-start | bytes 1769476
  3.0 2.8 %copy-start.6 = (bf16[20,1280]{1,0:T(8,128)(2,1)S(1)}, bf16[20,1280]{1,0:T(8,128)(2,1)}, u32[]{:S(2)}) copy-start(bf16[20,1280]{1,0:T(8,128)(2,1)} %param.31) | copy-start | bytes 153604
  3.0 3.5 %copy-start.5 = (bf16[20,1536]{1,0:T(8,128)(2,1)S(1)}, bf16[20,1536]{1,0:T(8,128)(2,1)}, u32[]{:S(2)}) copy-start(bf16[20,1536]{1,0:T(8,128)(2,1)} %param.27) | copy-start | bytes 184324
  3.0 4.1 %copy-start.7 = (bf16[1152,36]{0,1:T(8,128)(2,1)S(1)}, bf16[1152,36]{0,1:T(8,128)(2,1)}, u32[]{:S(2)}) copy-start(bf16[1152,36]{0,1:T(8,128)(2,1)} %param.21) | copy-start | bytes 248836
  7.2 2.1 %copy-start.8 = (bf16[40,640]{1,0:T(8,128)(2,1)S(1)}, bf16[40,640]{1,0:T(8,128)(2,1)}, u32[]{:S(2)}) copy-start(bf16[40,640]{1,0:T(8,128)(2,1)} %param.30) | copy-start | bytes 153604
  7.2 2.1 %copy-start.9 = (bf16[40,640]{1,0:T(8,128)(2,1)S(1)}, bf16[40,640]{1,0:T(8,128)(2,1)}, u32[]{:S(2)}) copy-start(bf16[40,640]{1,0:T(8,128)(2,1)} %param.28) | copy-start | bytes 153604
  7.2 2.1 %copy-start.10 = (bf16[40,640]{1,0:T(8,128)(2,1)S(1)}, bf16[40,640]{1,0:T(8,128)(2,1)}, u32[]{:S(2)}) copy-start(bf16[40,640]{1,0:T(8,128)(2,1)} %param.26) | copy-start | bytes 153604
  172.0 4.0 %copy-start.4 = (f32[40,768]{1,0:T(8,128)S(1)}, f32[40,768]{1,0:T(8,128)}, u32[]{:S(2)}) copy-start(f32[40,768]{1,0:T(8,128)} %get-tuple-element.14) | copy-start | bytes 368644
  172.0 5.0 %copy-start.3 = (f32[40,768]{1,0:T(8,128)S(1)}, f32[40,768]{1,0:T(8,128)}, u32[]{:S(2)}) copy-start(f32[40,768]{1,0:T(8,128)} %get-tuple-element.16) | copy-start | bytes 368644
  173.1 4.8 %copy-start.1 = (f32[24,1536]{1,0:T(8,128)S(1)}, f32[24,1536]{1,0:T(8,128)}, u32[]{:S(2)}) copy-start(f32[24,1536]{1,0:T(8,128)} %get-tuple-element.13) | copy-start | bytes 442372
  173.1 5.5 %copy-start.2 = (f32[24,1280]{1,0:T(8,128)S(1)}, f32[24,1280]{1,0:T(8,128)}, u32[]{:S(2)}) copy-start(f32[24,1280]{1,0:T(8,128)} %get-tuple-element.17) | copy-start | bytes 368644
where the time goes:
time: 179 us
  Pallas kernels  159 us (89%)
  local copies, waits for them, and re-layouts  10.6 us (6%)
  matrix products  6.93 us (4%)
  other arithmetic  2.17 us (1%)
    pallas_call x1, Pallas kernels, distil(): pl.pallas_call(functools.partial(kernel, factor), out_shape=outs + landin...  159 us
    dot_general x4, matrix products, place_columns(): jnp.dot(values, table, preferred_element_type=jnp.float32)  6.93 us
    unnamed x27, local copies, waits for them, and re-layouts  3.72 us

commit v1 on v0

--- a/solution.py
+++ b/solution.py
@@ -209,9 +209,27 @@
         return taken
 
 
+def mirror_flags(indices):
+    patch = lax.broadcasted_iota(jnp.int32, (8, 256), 1)
+    teacher = lax.broadcasted_iota(jnp.int32, (8, 256), 0)
+    flags = jnp.zeros((8, 256), jnp.float32)
+    for t, index in enumerate(indices):
+        same = (index[...] == patch).astype(jnp.float32)
+        flags = jnp.where(teacher == t, same, flags)
+    row = lax.broadcasted_iota(jnp.int32, (8, LANE), 0)
+    lane = lax.broadcasted_iota(jnp.int32, (8, LANE), 1)
+    turned = lax.dot_general(
+        flags.astype(jnp.bfloat16),
+        (row == lane).astype(jnp.bfloat16),
+        (((0,), (0,)), ((), ())),
+        preferred_element_type=jnp.float32,
+    )
+    return turned.astype(jnp.bfloat16)
+
+
 def kernel(factor, *refs):
     refs = Refs(refs)
-    shards, inputs, (feats, flags_in) = refs.take(9), refs.take(3), refs.take(2)
+    shards, inputs, (feats, *indices) = refs.take(9), refs.take(3), refs.take(4)
     outs, weights = refs.take(6), refs.take(6)
     hop_y, ((rows_y,), hop_x, (rows_all,), hop_z) = refs.take(2), (
         refs.take(1),
@@ -235,7 +253,7 @@
         .astype(jnp.bfloat16)
         .reshape(4, 4, 16, 1280)
     )
-    student_in[:, :, :, 1280:] = flags_in[...].reshape(4, 4, 16, LANE)
+    student_in[:, :, :, 1280:] = mirror_flags(indices).reshape(4, 4, 16, LANE)
     enter(
         [
             at.x_next(1),
@@ -684,7 +702,7 @@
     copies.finish()
 
 
-def distil(shards, inputs, feats, flags, factor):
+def distil(shards, inputs, feats, indices, factor):
     inside = pl.BlockSpec(memory_space=pltpu.VMEM)
     outside = pl.BlockSpec(memory_space=pl.ANY)
     depth = [40] * 3 + [24] * 3
@@ -725,7 +743,7 @@
     results = pl.pallas_call(
         functools.partial(kernel, factor),
         out_shape=outs + landings,
-        in_specs=[outside] * (len(shards) + len(inputs)) + [inside] * 2,
+        in_specs=[outside] * (len(shards) + len(inputs)) + [inside] * 4,
         out_specs=[inside] * len(outs) + [outside] * len(landings),
         scratch_shapes=[
             table(4, 4, 2, 48, 1536),
@@ -757,7 +775,7 @@
             collective_id=0, has_side_effects=True, vmem_limit_bytes=63 * 1024 * 1024
         ),
         name="distil",
-    )(*shards, *inputs, feats, flags)
+    )(*shards, *inputs, feats, *indices)
     return results[: len(outs)]
 
 
@@ -769,12 +787,6 @@
 
 def place_columns(values, table):
     return jnp.dot(values, table, preferred_element_type=jnp.float32).astype(jnp.bfloat16)
-
-
-def mirror_flags(indices):
-    patches = jnp.arange(256, dtype=jnp.int32)
-    flags = jnp.stack([index[0] == patches for index in indices], axis=-1).astype(jnp.bfloat16)
-    return jnp.pad(flags, ((0, 0), (0, LANE - 3)))
 
 
 def body(
@@ -814,7 +826,7 @@
             sam_in.reshape(1024, -1),
         ],
         student_feats[0],
-        mirror_flags((dino_index, siglip_index, sam_index)),
+        (dino_index, siglip_index, sam_index),
         2.0 / images_total,
     )
     firsts = [total.reshape(40, 32, 24)[..., :20].reshape(40, 640) for total in sums[:3]]

time: 179 us -> 177 us (0.989)
  other arithmetic: 2.17 us -> 0.05 us
where the time goes in v1:
time: 177 us
  Pallas kernels  159 us (90%)
  local copies, waits for them, and re-layouts  10.5 us (6%)
  matrix products  6.99 us (4%)
    pallas_call x1, Pallas kernels, distil(): pl.pallas_call(functools.partial(kernel, factor), out_shape=outs + landin...  159 us
    dot_general x4, matrix products, place_columns(): jnp.dot(values, table, preferred_element_type=jnp.float32)  6.99 us
    unnamed x27, local copies, waits for them, and re-layouts  3.73 us

profile of v1, /device:TPU:1, one launch (start us, length us, event | category | flops | bytes accessed | tf_op | source)
XLA Modules:
  0.0 177.1 jit_solution(14676367598753494578)
XLA Ops:
  0.6 0.0 copy-start
  0.7 0.0 copy-start.6
  0.7 0.0 copy-start.5
  0.8 0.0 copy-start.7
  0.8 2.2 %fusion.2 = bf16[20,1280]{1,0:T(8,128)(2,1)S(1)} fusion(bf16[20,1152]{1,0:T(8,128)(2,1)} %param.29, s32[1152]{0:T(1024)S(1)} %get-tuple-element.28, s32[1152]{0:T(1024)S(1)} %get-tuple-element.29, s32[1152]{0:T(1024)S(1)} %get-tuple-element.27, s32[1152]{0:T(1024)S(1)} %get-tuple-element.30, pred[1152]{0:T(1024)(128)(4,1)S(1)} %get-tuple-element.31, ...), kind=kOutput, calls=%fused_computation.6 | convolution fusion | flops 66380800 | bytes 118016 | tf_op jit(solution)/shard_map/dot_general | solution.py:789
  3.0 0.6 pad.17.refs_7_
  3.7 0.0 copy-done.6
  3.7 0.6 pad.18.refs_8_
  4.3 0.0 copy-done.5
  4.3 0.6 pad.16.refs_6_
  4.9 0.0 copy-done.7
  4.9 0.0 copy-start.8
  4.9 0.0 copy-start.9
  4.9 0.0 copy-start.10
  4.9 1.4 fusion.1
  6.3 0.7 pad.15.refs_1_
  7.0 0.0 copy-done.8
  7.0 0.0 copy-done.9
  7.0 0.0 copy-done.10
  7.0 0.8 fusion.4
  7.8 0.7 fusion.32
  8.5 0.0 copy-done
  8.5 2.5 %fusion.refs_10_ = bf16[256,1280]{1,0:T(8,128)(2,1)} fusion(bf16[32,8,1152]{2,1,0:T(8,128)(2,1)S(1)} %copy-done, s32[1152]{0:T(1024)S(1)} %get-tuple-element.28, s32[1152]{0:T(1024)S(1)} %get-tuple-element.29, s32[1152]{0:T(1024)S(1)} %get-tuple-element.27, s32[1152]{0:T(1024)S(1)} %get-tuple-element.30, pred[1152]{0:T(1024)(128)(4,1)S(1)} %get-tuple-element.31, ...), kind=kOutput, calls=%fused_computation.2 | convolution fusion | flops 762675200 | bytes 1265920 | tf_op jit(solution)/shard_map/dot_general | solution.py:789
  11.0 158.7 %distil.1 = (f32[40,768]{1,0:T(8,128)}, f32[40,768]{1,0:T(8,128)}, f32[40,768]{1,0:T(8,128)}, f32[24,1536]{1,0:T(8,128)}, f32[24,1280]{1,0:T(8,128)}, /*index=5*...) custom-call(bf16[48,1536]{1,0:T(8,128)(2,1)} %bitcast.39, ...), custom_call_target="tpu_custom_call" | custom-call | tf_op jit(solution)/shard_map/distil/pallas_call | solution.py:743
  169.8 0.0 copy-start.4
  169.8 0.0 copy-start.3
  169.8 1.1 copy.24
  170.9 0.0 copy-start.1
  171.0 0.0 copy-start.2
  171.0 0.8 copy.27
  171.8 1.1 reshape.59
  172.9 0.9 reshape.60
  173.8 0.0 copy-done.4
  173.8 0.2 copy.25
  174.0 0.8 copy.28
  174.7 0.0 copy-done.3
  174.7 0.2 copy.26
  175.0 0.8 copy.29
  175.7 0.0 copy-done.1
  175.7 0.7 copy.33
  176.4 0.0 copy-done.2
  176.4 0.6 copy.34
  (9 shorter events, 0.1 us)
Async XLA Ops:
  0.6 7.9 %copy-start = (bf16[32,8,1152]{2,1,0:T(8,128)(2,1)S(1)}, bf16[32,8,1152]{2,1,0:T(8,128)(2,1)}, u32[]{:S(2)}) copy-start(bf16[32,8,1152]{2,1,0:T(8,128)(2,1)} %param.18) | copy-start | bytes 1769476
  0.7 2.9 %copy-start.6 = (bf16[20,1280]{1,0:T(8,128)(2,1)S(1)}, bf16[20,1280]{1,0:T(8,128)(2,1)}, u32[]{:S(2)}) copy-start(bf16[20,1280]{1,0:T(8,128)(2,1)} %param.31) | copy-start | bytes 153604
  0.7 3.5 %copy-start.5 = (bf16[20,1536]{1,0:T(8,128)(2,1)S(1)}, bf16[20,1536]{1,0:T(8,128)(2,1)}, u32[]{:S(2)}) copy-start(bf16[20,1536]{1,0:T(8,128)(2,1)} %param.27) | copy-start | bytes 184324
  0.8 4.2 %copy-start.7 = (bf16[1152,36]{0,1:T(8,128)(2,1)S(1)}, bf16[1152,36]{0,1:T(8,128)(2,1)}, u32[]{:S(2)}) copy-start(bf16[1152,36]{0,1:T(8,128)(2,1)} %param.21) | copy-start | bytes 248836
  4.9 2.1 %copy-start.8 = (bf16[40,640]{1,0:T(8,128)(2,1)S(1)}, bf16[40,640]{1,0:T(8,128)(2,1)}, u32[]{:S(2)}) copy-start(bf16[40,640]{1,0:T(8,128)(2,1)} %param.30) | copy-start | bytes 153604
  4.9 2.1 %copy-start.9 = (bf16[40,640]{1,0:T(8,128)(2,1)S(1)}, bf16[40,640]{1,0:T(8,128)(2,1)}, u32[]{:S(2)}) copy-start(bf16[40,640]{1,0:T(8,128)(2,1)} %param.28) | copy-start | bytes 153604
  4.9 2.1 %copy-start.10 = (bf16[40,640]{1,0:T(8,128)(2,1)S(1)}, bf16[40,640]{1,0:T(8,128)(2,1)}, u32[]{:S(2)}) copy-start(bf16[40,640]{1,0:T(8,128)(2,1)} %param.26) | copy-start | bytes 153604
  169.8 4.0 %copy-start.4 = (f32[40,768]{1,0:T(8,128)S(1)}, f32[40,768]{1,0:T(8,128)}, u32[]{:S(2)}) copy-start(f32[40,768]{1,0:T(8,128)} %get-tuple-element.14) | copy-start | bytes 368644
  169.8 5.0 %copy-start.3 = (f32[40,768]{1,0:T(8,128)S(1)}, f32[40,768]{1,0:T(8,128)}, u32[]{:S(2)}) copy-start(f32[40,768]{1,0:T(8,128)} %get-tuple-element.16) | copy-start | bytes 368644
  170.9 4.8 %copy-start.1 = (f32[24,1536]{1,0:T(8,128)S(1)}, f32[24,1536]{1,0:T(8,128)}, u32[]{:S(2)}) copy-start(f32[24,1536]{1,0:T(8,128)} %get-tuple-element.13) | copy-start | bytes 442372
  171.0 5.5 %copy-start.2 = (f32[24,1280]{1,0:T(8,128)S(1)}, f32[24,1280]{1,0:T(8,128)}, u32[]{:S(2)}) copy-start(f32[24,1280]{1,0:T(8,128)} %get-tuple-element.17) | copy-start | bytes 368644
